TPU v7x, 256 devices: a whole 4x4x8 slice. The times are simulated.
256 devices in a mesh: grp: 16 (over x, y_lo, core), seq: 16 (over z, y_hi).
Axes of the slice: x: 4, y: 4 (y_hi: 2, y_lo: 2; y = y_hi * 2 + y_lo), z: 8, core: 2. Of those that a mesh axis runs over, the one named last changes fastest.
Arguments:
- queries: bfloat16 [16, 3072, 2048], P('grp', 'seq'), may hold values from -24 to 24
- template_suffix_keys: bfloat16 [16, 3072, 1024], P('grp', 'seq'), may hold values from -6 to 6
- template_suffix_values: bfloat16 [16, 3072, 1024], P('grp', 'seq'), may hold values from -6 to 6
- cached_prefix_keys: bfloat16 [4096, 1024], P('grp'), may hold values from -9 to 9
- cached_prefix_values: bfloat16 [4096, 1024], P('grp'), may hold values from -6 to 6
- lengths: int32 [16], P('grp'), may hold values from 192 to 3072, as said below
Outputs:
- attended: bfloat16 [16, 3072, 2048], P('grp', 'seq')
Inputs may be any that keep to these rules, and one draw needn't show every extreme that they name: `lengths`: some template has length 3072.
All inputs are finite; a program needn't handle non-finite values.
Results may differ from a plain program's by a relative error of at most 0.018.
Values may be sent and summed in bfloat16 or wider, within the bound.
No kernel may reach another device: no remote copies, remote signals or barrier semaphores. Data moves between devices by JAX's collectives and lax.ppermute only.
A program may use at most 256 MiB of HBM per device.

v0:
```python
import jax
import jax.numpy as jnp
from jax import lax
from jax.sharding import PartitionSpec as P

HQ = 16
LOCAL_KV_HEADS = 8
HEAD_SIZE = 128
QUERY_PER_KV = 2


query_scale = 168.0 ** (-0.5)


def attend(running, query_slab, key_slab, value_slab, visible):
    row_peak, row_total, row_accum = running
    heads_of_keys = key_slab.reshape(-1, LOCAL_KV_HEADS, HEAD_SIZE)
    heads_of_values = value_slab.reshape(-1, LOCAL_KV_HEADS, HEAD_SIZE)
    scores = (
        jnp.einsum("rkgd,nkd->kgrn", query_slab, heads_of_keys, preferred_element_type=jnp.float32)
        * query_scale
    )
    if visible is not None:
        scores = jnp.where(visible, scores, jnp.float32(-1e30))
    new_peak = jnp.maximum(row_peak, jnp.max(scores, axis=-1))
    factor = jnp.exp(row_peak - new_peak)
    weights = jnp.exp(scores - new_peak[..., None])
    row_total = row_total * factor + jnp.sum(weights, axis=-1)
    added = jnp.einsum(
        "kgrn,nkd->kgrd",
        weights.astype(jnp.bfloat16),
        heads_of_values,
        preferred_element_type=jnp.float32,
    )
    row_accum = row_accum * factor[..., None] + added
    return (new_peak, row_total, row_accum)


def on_device(
    queries,
    template_suffix_keys,
    template_suffix_values,
    cached_prefix_keys,
    cached_prefix_values,
    lengths,
):
    count_of_rows = queries.shape[1]
    query_slab = queries[0].reshape(count_of_rows, LOCAL_KV_HEADS, QUERY_PER_KV, HEAD_SIZE)
    first_row = lax.axis_index("seq") * count_of_rows
    suffix_length = lengths[0]
    row_ids = first_row + jnp.arange(count_of_rows, dtype=jnp.int32)
    initial = (
        jnp.full((LOCAL_KV_HEADS, QUERY_PER_KV, count_of_rows), -1e30, jnp.float32),
        jnp.zeros((LOCAL_KV_HEADS, QUERY_PER_KV, count_of_rows), jnp.float32),
        jnp.zeros((LOCAL_KV_HEADS, QUERY_PER_KV, count_of_rows, HEAD_SIZE), jnp.float32),
    )
    panels = (
        lax.all_gather(cached_prefix_keys, "grp", axis=0, tiled=True),
        lax.all_gather(cached_prefix_values, "grp", axis=0, tiled=True),
    )
    running = attend(initial, query_slab, panels[0], panels[1], None)
    panels = (
        lax.all_gather(template_suffix_keys[0], "seq", axis=0, tiled=True),
        lax.all_gather(template_suffix_values[0], "seq", axis=0, tiled=True),
    )
    block_rows = panels[0].shape[0]
    key_ids = jnp.arange(block_rows, dtype=jnp.int32)
    visible = key_ids[None, :] <= row_ids[:, None]
    running = attend(running, query_slab, panels[0], panels[1], visible)
    row_peak, row_total, row_accum = running
    result = row_accum / row_total[..., None]
    result = jnp.transpose(result, (2, 0, 1, 3)).reshape(count_of_rows, HQ * HEAD_SIZE)
    live_rows = row_ids < suffix_length
    result = jnp.where(live_rows[:, None], result, jnp.float32(0.0)).astype(jnp.bfloat16)
    return result[None]


def solution(mesh):
    in_specs = (
        P("grp", "seq", None),
        P("grp", "seq", None),
        P("grp", "seq", None),
        P("grp", None),
        P("grp", None),
        P("grp"),
    )
    out_specs = P("grp", "seq", None)
    return jax.shard_map(
        on_device, mesh=mesh, in_specs=in_specs, out_specs=out_specs, check_vma=False
    )
```

profile of v0, /device:TPU:16, one launch (start us, length us, event | category | flops | bytes accessed | tf_op | source)
XLA Modules:
  0.0 436.1 jit_solution(13073291108143285848)
XLA Ops:
  6.5 0.7 all-gather.11.cloned.1.call-update
  7.3 0.0 all-gather.13.cloned.1.call-start
  7.3 0.7 all-gather.13.cloned.1.call-update
  8.0 0.0 all-gather.7.cloned.1.call-start
  8.1 2.0 copy.20
  10.1 0.0 all-gather.9.cloned.1.call-start
  10.2 2.0 copy.23
  12.2 2.6 reshape_squeeze.3
  15.5 0.4 iota_compare_fusion
  15.9 110.2 %all-gather.11.cloned.1.call-done = bf16[1,3072,1024]{2,1,0:T(8,128)(2,1)} async-done(((bf16[1,192,1024]{2,1,0:T(8,128)(2,1)}), bf16[1,3072,1024]{2,1,0:T(8,128)(2,1)}) %all-gather.11.cloned.1.call-update) | async-done | bytes 6291472 | tf_op jit(solution)/shard_map/all_gather | solution.py:63
  126.1 8.7 %copy.25 = bf16[1,3072,1024]{1,2,0:T(8,128)(2,1)} copy(bf16[1,3072,1024]{2,1,0:T(8,128)(2,1)} %all-gather.11.cloned.1.call-done) | data formatting | bytes 12582912 | tf_op jit(solution)/shard_map/all_gather | solution.py:63
  134.7 106.6 %all-gather.13.cloned.1.call-done = bf16[1,3072,1024]{2,1,0:T(8,128)(2,1)} async-done(((bf16[1,192,1024]{2,1,0:T(8,128)(2,1)}), bf16[1,3072,1024]{2,1,0:T(8,128)(2,1)}) %all-gather.13.cloned.1.call-update) | async-done | bytes 6291472 | tf_op jit(solution)/shard_map/all_gather | solution.py:64
  241.4 8.7 %copy.28 = bf16[1,3072,1024]{1,2,0:T(8,128)(2,1)} copy(bf16[1,3072,1024]{2,1,0:T(8,128)(2,1)} %all-gather.13.cloned.1.call-done) | data formatting | bytes 12582912 | tf_op jit(solution)/shard_map/all_gather | solution.py:64
  250.1 17.9 %fusion.5 = (f32[8,2,192]{2,1,0:T(2,128)S(1)}, f32[8,3072,192,2]{1,2,3,0:T(8,128)}) fusion(pred[192,3072]{1,0:T(8,128)(4,1)S(1)} %iota_compare_fusion, bf16[3072,8,128,1]{0,2,3,1:T(8,128)(2,1)} %bitcast.78, bf16[192,8,2,128]{3,2,1,0:T(2,128)(2,1)S(1)} %reshape_squeeze.3), kind=kOutput, calls=%fused_computation.9 | convolution fusion | flops 2444227584 | bytes 45428736 | tf_op jit(solution)/shard_map/rkgd,nkd->kgrn/dot_general | solution.py:20
  267.9 37.0 %all-gather.7.cloned.1.call-done = bf16[4096,1024]{0,1:T(8,128)(2,1)} async-done(((bf16[256,1024]{0,1:T(8,128)(2,1)}), bf16[4096,1024]{0,1:T(8,128)(2,1)}) %all-gather.7.cloned.1.call-update) | async-done | bytes 8388624 | tf_op jit(solution)/shard_map/all_gather | solution.py:58
  304.9 21.5 %bitcast_reduce_fusion = (f32[8,2,192]{2,1,0:T(2,128)S(1)}, f32[8,4096,192,2]{1,2,3,0:T(8,128)}) fusion(bf16[4096,8,128,1]{0,2,3,1:T(8,128)(2,1)} %bitcast.80, bf16[192,8,2,128]{3,2,1,0:T(2,128)(2,1)S(1)} %reshape_squeeze.3), kind=kOutput, calls=%fused_computation.1 | convolution fusion | flops 3246388224 | bytes 59518976 | tf_op jit(solution)/shard_map/rkgd,nkd->kgrn/dot_general | solution.py:20
  326.5 21.3 %fusion.1 = f32[8,2,192]{2,1,0:T(2,128)S(1)} fusion(f32[8,4096,192,2]{1,2,3,0:T(8,128)} %get-tuple-element.13, f32[8,2,192]{2,1,0:T(2,128)S(1)} %get-tuple-element.9), kind=kLoop, calls=%fused_computation.3 | loop fusion | flops 37745664 | bytes 50356224 | tf_op jit(solution)/shard_map/reduce_sum | solution.py:28
  347.8 21.8 %all-gather.9.cloned.1.call-done = bf16[4096,1024]{0,1:T(8,128)(2,1)} async-done(((bf16[256,1024]{0,1:T(8,128)(2,1)}), bf16[4096,1024]{0,1:T(8,128)(2,1)}) %all-gather.9.cloned.1.call-update) | async-done | bytes 8388624 | tf_op jit(solution)/shard_map/all_gather | solution.py:59
  369.6 21.9 %fusion.6 = f32[8,2,192,128]{3,2,1,0:T(8,128)S(1)} fusion(bf16[4096,8,128,1]{0,2,3,1:T(8,128)(2,1)} %bitcast.79, f32[8,4096,192,2]{1,2,3,0:T(8,128)} %get-tuple-element.13, f32[8,2,192]{2,1,0:T(2,128)S(1)} %get-tuple-element.9), kind=kOutput, calls=%fused_computation.10 | convolution fusion | flops 3258974208 | bytes 60305408 | tf_op jit(solution)/shard_map/kgrn,nkd->kgrd/dot_general | solution.py:29
  391.5 17.1 %fusion.3 = f32[8,2,192]{2,1,0:T(2,128)S(1)} fusion(f32[8,3072,192,2]{1,2,3,0:T(8,128)} %get-tuple-element.11, f32[8,2,192]{2,1,0:T(2,128)S(1)} %get-tuple-element.8, pred[192,3072]{1,0:T(8,128)(4,1)S(1)} %iota_compare_fusion), kind=kLoop, calls=%fused_computation.7 | loop fusion | flops 37745664 | bytes 38363136 | tf_op jit(solution)/shard_map/reduce_sum | solution.py:28
  408.6 18.5 %fusion.13 = bf16[192,8,2,128]{3,0,2,1:T(8,128)(2,1)S(1)} fusion(f32[8,2,192,128]{3,2,1,0:T(8,128)S(1)} %fusion.6, bf16[3072,8,128,1]{0,2,3,1:T(8,128)(2,1)} %bitcast.81, f32[8,3072,192,2]{1,2,3,0:T(8,128)} %get-tuple-element.11, f32[8,2,192]{2,1,0:T(2,128)S(1)} %get-tuple-element.8, pred[192,3072]{1,0:T(8,128)(4,1)S(1)} %iota_compare_fusion, ...), kind=kOutput, calls=%fused_computation.17 | convolution fusion | flops 2455633920 | bytes 47038464 | tf_op jit(solution)/shard_map/kgrn,nkd->kgrd/dot_general | solution.py:29
  427.1 0.8 copy.30
  427.9 0.6 reshape.88
  428.5 1.1 select_convert_fusion
  (7 shorter events, 0.1 us)
Async XLA Ops:
  6.5 119.5 %all-gather.11.cloned.1.call-start = ((), (), s32[]{:S(2)}) async-start(), calls=%async_computation.2 | async-start | bytes 6684672 | tf_op jit(solution)/shard_map/all_gather | solution.py:63
  7.3 234.1 %all-gather.13.cloned.1.call-start = ((), (), s32[]{:S(2)}) async-start(), calls=%async_computation.3 | async-start | bytes 6684672 | tf_op jit(solution)/shard_map/all_gather | solution.py:64
  8.0 296.9 %all-gather.7.cloned.1.call-start = ((), (), s32[]{:S(2)}) async-start(), calls=%async_computation | async-start | bytes 8912896 | tf_op jit(solution)/shard_map/all_gather | solution.py:58
  10.1 359.5 %all-gather.9.cloned.1.call-start = ((), (), s32[]{:S(2)}) async-start(), calls=%async_computation.1 | async-start | bytes 8912896 | tf_op jit(solution)/shard_map/all_gather | solution.py:59
Sparse Core Ops, SparseCore 0:
  9.9 116.0 all-gather.10
  128.7 112.6 all-gather.12
  243.2 61.7 all-gather.6
  306.6 62.9 all-gather.8
where the time goes:
time: 440 us; the launch traced here: 436 us
  waiting for transfers between devices  277 us (63%)
  matrix products  79.7 us (18%)
  other arithmetic  39.9 us (9%)
  local copies, waits for them, and re-layouts  25.4 us (6%)
  between operations  13.9 us (3%)
    all_gather x1, waiting for transfers between devices, on_device(): lax.all_gather(template_suffix_keys[0], 'seq', axis=0, tiled=True)  110 us
    all_gather x1, waiting for transfers between devices, on_device(): lax.all_gather(template_suffix_values[0], 'seq', axis=0, tiled=True)  107 us
    dot_general x2, matrix products, attend(): jnp.einsum('kgrn,nkd->kgrd', weights.astype(jnp.bfloat16), heads_of_value...  40.4 us
    dot_general x2, matrix products, attend(): jnp.einsum('rkgd,nkd->kgrn', query_slab, heads_of_keys, preferred_element...  39.4 us
    reduce_sum x2, other arithmetic, attend(): row_total = row_total * factor + jnp.sum(weights, axis=-1)  38.3 us
    all_gather x1, waiting for transfers between devices, on_device(): lax.all_gather(cached_prefix_keys, 'grp', axis=0, tiled=True)  37 us
    all_gather x1, waiting for transfers between devices, on_device(): lax.all_gather(cached_prefix_values, 'grp', axis=0, tiled=True)  21.8 us
  transfers between devices with their start and end apart: 4, of which 4 were waited for; matrix products, arithmetic and copies ran while one was open for 20% of the time, Pallas kernels for 0%

commit v1 on v0

v1 whole, which is shorter than its diff:
```python
import jax
import jax.numpy as jnp
from jax import lax
from jax.experimental import pallas as pl
from jax.experimental.pallas import tpu as pltpu
from jax.sharding import Mesh, PartitionSpec as P

LOCAL_KV_HEADS = 8
HEAD_SIZE = 128
QUERY_PER_KV = 2
ROWS = 192
BLOCKS = 8
ALL_ROWS = BLOCKS * ROWS
PREFIX_HALF = 2048
ROW_TILE = 384
KEY_TILE = 512

query_scale = 168.0 ** (-0.5)
log2_e = 1.4426950408889634
total_bound = 1e37
hs = HEAD_SIZE
q_lanes = slice(0, 2 * hs)
k_lanes = slice(2 * hs, 3 * hs)
v_lanes = slice(3 * hs, 4 * hs)


def scores_of(query_pair, keys):
    return lax.dot_general(
        query_pair,
        jnp.concatenate([keys, keys], axis=1),
        (((1,), (1,)), ((), ())),
        preferred_element_type=jnp.float32,
    )


def weights_of(scores, shift):
    return jnp.exp2(scores - jnp.concatenate([shift] * (scores.shape[1] // 128), axis=1))


def summed_of(weights, values):
    return lax.dot_general(
        weights.astype(jnp.bfloat16),
        jnp.concatenate([values, jnp.ones_like(values)], axis=1),
        (((1,), (0,)), ((), ())),
        preferred_element_type=jnp.float32,
    )


def pair_of(queries):
    queries = jnp.concatenate([queries[:, 0:hs], queries[:, hs : 2 * hs]], axis=0)
    scaled = queries.astype(jnp.float32) * (query_scale * log2_e)
    high = scaled.astype(jnp.bfloat16)
    low = (scaled - high.astype(jnp.float32)).astype(jnp.bfloat16)
    return jnp.concatenate([high, low], axis=1)


def prefix_kernel(mine, prefix_a, prefix_b, shifts, accum):
    tiles = [(p, i) for p in (prefix_a, prefix_b) for i in range(0, PREFIX_HALF, KEY_TILE)]

    @pl.loop(0, ALL_ROWS // ROW_TILE)
    def _(step):
        rows = pl.ds(pl.multiple_of(step * ROW_TILE, ROW_TILE), ROW_TILE)
        pair = pair_of(mine[rows, q_lanes])
        first = scores_of(pair, prefix_a[0:256, 0:hs])
        shift = jnp.broadcast_to(jnp.max(first, axis=1, keepdims=True), (2 * ROW_TILE, 128))
        scores = scores_of(pair, prefix_a[0:KEY_TILE, 0:hs])
        total = None
        for j, (ref, start) in enumerate(tiles):
            following = None
            if j + 1 < len(tiles):
                next_ref, next_start = tiles[j + 1]
                following = scores_of(pair, next_ref[next_start : next_start + KEY_TILE, 0:hs])
            added = summed_of(weights_of(scores, shift), ref[start : start + KEY_TILE, hs : 2 * hs])
            total = added if total is None else total + added
            scores = following
        for member in range(QUERY_PER_KV):
            part = slice(member * ROW_TILE, (member + 1) * ROW_TILE)
            shifts[member, rows, :] = shift[part]
            accum[member, rows, :] = total[part]


def suffix_kernel(meta, mine, other, shifts, accum, prefix_a, prefix_b, out, peaks, again):
    second = meta[0]
    length = meta[1]
    row_ids = lax.broadcasted_iota(jnp.int32, (2 * ROWS, 2 * ROWS), 0)
    row_ids = jnp.where(row_ids < ROWS, row_ids, row_ids - ROWS)
    col_ids = lax.broadcasted_iota(jnp.int32, (2 * ROWS, 2 * ROWS), 1)
    visible = ((col_ids < ROWS) & (col_ids <= row_ids)) | ((col_ids >= ROWS) & (second == 1))

    def keys_of(block, which):
        parts = []
        if block > 0:
            parts += [mine[0 : block * ROWS, (k_lanes, v_lanes)[which]]]
            parts += [other[0 : block * ROWS, which * hs : (which + 1) * hs]]
        rows = slice(block * ROWS, (block + 1) * ROWS)
        parts += [mine[rows, (k_lanes, v_lanes)[which]]]
        parts += [other[rows, which * hs : (which + 1) * hs]]
        return jnp.concatenate(parts, axis=0)

    def both(ref, block):
        return jnp.concatenate([ref[m, block * ROWS : (block + 1) * ROWS, :] for m in range(2)], axis=0)

    def suffix_scores(block):
        return scores_of(pair_of(mine[block * ROWS : (block + 1) * ROWS, q_lanes]), keys_of(block, 0))

    def finish(block, total):
        result = total[:, 0:hs] / total[:, hs : 2 * hs]
        result = jnp.concatenate([result[0:ROWS], result[ROWS : 2 * ROWS]], axis=1)
        row = lax.broadcasted_iota(jnp.int32, (ROWS, 2 * hs), 0)
        live = (2 * block + second) * ROWS + row < length
        return jnp.where(live, result, 0.0).astype(jnp.bfloat16)

    scores = suffix_scores(0)
    beyond = jnp.zeros((2 * ROWS, hs), jnp.float32)
    for block in range(BLOCKS):
        following = suffix_scores(block + 1) if block + 1 < BLOCKS else None
        weights = weights_of(scores, both(shifts, block))
        edge = 2 * ROWS * block
        masked = jnp.where(visible, weights[:, edge:], 0.0)
        weights = jnp.concatenate([weights[:, :edge], masked], axis=1) if block > 0 else masked
        total = both(accum, block) + summed_of(weights, keys_of(block, 1))
        beyond = jnp.maximum(beyond, jnp.where(total[:, hs:] < total_bound, 0.0, 1.0))
        out[block * ROWS : (block + 1) * ROWS, :] = finish(block, total)
        scores = following

    @pl.when(jnp.max(beyond) > 0.0)
    def _():
        @pl.loop(0, BLOCKS)
        def _(block):
            rows = pl.ds(pl.multiple_of(block * ROWS, ROWS), ROWS)
            pair = pair_of(mine[rows, q_lanes])
            peaks[...] = jnp.full((2 * ROWS, 128), -1e30, jnp.float32)
            again[...] = jnp.zeros((2 * ROWS, 2 * hs), jnp.float32)

            def step(keys, values, seen):
                part = scores_of(pair, keys)
                if seen is not None:
                    part = jnp.where(seen, part, -1e30)
                old = peaks[:, 0:1]
                new = jnp.maximum(old, jnp.max(part, axis=1, keepdims=True))
                weights = jnp.exp2(part - new)
                again[...] = again[...] * jnp.exp2(old - new) + summed_of(weights, values)
                peaks[...] = jnp.broadcast_to(new, (2 * ROWS, 128))

            for ref in (prefix_a, prefix_b):

                @pl.loop(0, PREFIX_HALF // 256)
                def _(i):
                    keys = pl.ds(pl.multiple_of(i * 256, 256), 256)
                    step(ref[keys, 0:hs], ref[keys, hs : 2 * hs], None)

            row = lax.broadcasted_iota(jnp.int32, (2 * ROWS, ROWS), 0)
            row = jnp.where(row < ROWS, row, row - ROWS)
            col = lax.broadcasted_iota(jnp.int32, (2 * ROWS, ROWS), 1)

            @pl.loop(0, block + 1)
            def _(i):
                keys = pl.ds(pl.multiple_of(i * ROWS, ROWS), ROWS)
                step(mine[keys, k_lanes], mine[keys, v_lanes], (col <= row) | (i < block))
                full = (i < block) | (second == 1)
                step(other[keys, 0:hs], other[keys, hs : 2 * hs], (col >= 0) & full)

            out[rows, :] = finish(block, again[...])


in_vmem = pl.BlockSpec(memory_space=pltpu.VMEM)


def prefix_part(mine, prefix_a, prefix_b):
    count = 2 * ALL_ROWS * 2 * PREFIX_HALF
    return pl.pallas_call(
        prefix_kernel,
        out_shape=(
            jax.ShapeDtypeStruct((2, ALL_ROWS, 128), jnp.float32),
            jax.ShapeDtypeStruct((2, ALL_ROWS, 2 * hs), jnp.float32),
        ),
        in_specs=[in_vmem] * 3,
        out_specs=(in_vmem, in_vmem),
        compiler_params=pltpu.CompilerParams(vmem_limit_bytes=24 << 20),
        cost_estimate=pl.CostEstimate(
            flops=count * 256 * 4, bytes_accessed=8 << 20, transcendentals=count
        ),
    )(mine, prefix_a, prefix_b)


def suffix_part(meta, mine, other, shifts, accum, prefix_a, prefix_b):
    count = 2 * ALL_ROWS * ALL_ROWS
    return pl.pallas_call(
        suffix_kernel,
        out_shape=jax.ShapeDtypeStruct((ALL_ROWS, 2 * hs), jnp.bfloat16),
        in_specs=[pl.BlockSpec(memory_space=pltpu.SMEM)] + [in_vmem] * 6,
        out_specs=in_vmem,
        scratch_shapes=[
            pltpu.VMEM((2 * ROWS, 128), jnp.float32),
            pltpu.VMEM((2 * ROWS, 2 * hs), jnp.float32),
        ],
        compiler_params=pltpu.CompilerParams(vmem_limit_bytes=28 << 20),
        cost_estimate=pl.CostEstimate(
            flops=count * 256 * 4, bytes_accessed=8 << 20, transcendentals=count
        ),
    )(meta, mine, other, shifts, accum, prefix_a, prefix_b)


def split_kernel(queries, keys, values, out):
    for head in range(LOCAL_KV_HEADS):
        out[head, :, q_lanes] = queries[:, 2 * head * hs : 2 * (head + 1) * hs]
        out[head, :, k_lanes] = keys[:, head * hs : (head + 1) * hs]
        out[head, :, v_lanes] = values[:, head * hs : (head + 1) * hs]


def join_kernel(by_head, out):
    for head in range(LOCAL_KV_HEADS):
        out[:, 2 * head * hs : 2 * (head + 1) * hs] = by_head[head]


def relaid(kernel, shape, *operands):
    return pl.pallas_call(
        kernel,
        out_shape=jax.ShapeDtypeStruct(shape, jnp.bfloat16),
        in_specs=[in_vmem] * len(operands),
        out_specs=in_vmem,
        compiler_params=pltpu.CompilerParams(vmem_limit_bytes=12 << 20),
    )(*operands)


def on_device(queries, suffix_keys, suffix_values, prefix_keys, prefix_values, lengths):
    head = lax.axis_index("z")
    second = lax.axis_index("yh").astype(jnp.int32)
    meta = jnp.stack([second, lengths[0]])

    def swapped(array, axis):
        return lax.ppermute(array, axis, [(0, 1), (1, 0)])

    mine = relaid(
        split_kernel,
        (LOCAL_KV_HEADS, ROWS, 4 * hs),
        queries[0],
        suffix_keys[0],
        suffix_values[0],
    )
    mine = lax.all_to_all(mine, "z", 0, 0, tiled=False).reshape(ALL_ROWS, 4 * hs)
    other = swapped(mine[:, 2 * hs :], "yh")

    part = jnp.concatenate(
        [
            lax.dynamic_slice_in_dim(prefix_keys, head * hs, hs, axis=1),
            lax.dynamic_slice_in_dim(prefix_values, head * hs, hs, axis=1),
        ],
        axis=1,
    )
    column = jnp.concatenate(
        [part]
        + [lax.ppermute(part, "x", [(i, (i + shift) % 4) for i in range(4)]) for shift in (1, 3, 2)],
        axis=0,
    )
    prefix_a = jnp.concatenate([column, swapped(column, "yl")], axis=0)
    prefix_b = swapped(prefix_a, "core")

    shifts, accum = prefix_part(mine, prefix_a, prefix_b)
    attended = suffix_part(meta, mine, other, shifts, accum, prefix_a, prefix_b)
    attended = lax.all_to_all(attended.reshape(BLOCKS, ROWS, 2 * hs), "z", 0, 0, tiled=False)
    return relaid(join_kernel, (ROWS, LOCAL_KV_HEADS * 2 * hs), attended)[None]


def solution(mesh):
    fine = Mesh(mesh.devices.reshape(4, 2, 2, 8, 2), ("x", "yl", "core", "z", "yh"))
    grp, seq = ("x", "yl", "core"), ("z", "yh")
    in_specs = (
        P(grp, seq, None),
        P(grp, seq, None),
        P(grp, seq, None),
        P(grp, None),
        P(grp, None),
        P(grp),
    )
    return jax.shard_map(
        on_device, mesh=fine, in_specs=in_specs, out_specs=P(grp, seq, None), check_vma=False
    )
```

time: 440 us -> 246 us (0.56)
  waiting for transfers between devices: 277 us -> 32 us
  Pallas kernels: 0 us -> 166 us
  matrix products: 79.7 us -> 0 us
  other arithmetic: 39.9 us -> 0.14 us
  blocking collectives: 0 us -> 25.8 us
  local copies, waits for them, and re-layouts: 25.4 us -> 4.12 us
  starting transfers between devices: 0.12 us -> 15.7 us
  between operations: 13.9 us -> 0.73 us
    all_gather x4 -> x0, waiting for transfers between devices: 276 us -> none  [the longest x1 110 us: on_device(): lax.all_gather(template_suffix_keys[0], 'seq', axis=0, tiled=True)]
    pallas_call x0 -> x4, Pallas kernels: none -> 166 us  [the longest x1 146 us: suffix_part(): pl.pallas_call(suffix_kernel, out_shape=jax.ShapeDtypeStruct((ALL_ROWS, 2...]
    dot_general x4 -> x0, matrix products: 79.7 us -> none  [the longest x2 40.4 us: attend(): jnp.einsum('kgrn,nkd->kgrd', weights.astype(jnp.bfloat16), heads_of_value...]
    reduce_sum x2 -> x0, other arithmetic: 38.3 us -> none  [attend(): row_total = row_total * factor + jnp.sum(weights, axis=-1)]
    all_to_all x0 -> x1, blocking collectives: none -> 25.8 us  [on_device(): lax.all_to_all(attended.reshape(BLOCKS, ROWS, 2 * hs), 'z', 0, 0, tiled=F...]
    all_gather x2 -> x0, local copies, waits for them, and re-layouts: 17.3 us -> none  [the longest x1 8.69 us: on_device(): lax.all_gather(template_suffix_values[0], 'seq', axis=0, tiled=True)]
    ppermute x0 -> x6, waiting for transfers between devices: none -> 17.1 us  [the longest x3 10.7 us: swapped(): return lax.ppermute(array, axis, [(0, 1), (1, 0)])]
    all_to_all x0 -> x1, waiting for transfers between devices: none -> 14.9 us  [on_device(): lax.all_to_all(mine, 'z', 0, 0, tiled=False).reshape(ALL_ROWS, 4 * hs)]
  transfers between devices with their start and end apart: 4 -> 7, of which waited for: 4 -> 5; matrix products, arithmetic and copies ran while one was open for 20% -> 0% of each run, Pallas kernels for 0% -> 7%
where the time goes in v1:
time: 246 us; the launch traced here: 244 us
  Pallas kernels  166 us (67%)
  waiting for transfers between devices  32 us (13%)
  blocking collectives  25.8 us (10%)
  starting transfers between devices  15.7 us (6%)
  local copies, waits for them, and re-layouts  4.12 us (2%)
    pallas_call x1, Pallas kernels, suffix_part(): pl.pallas_call(suffix_kernel, out_shape=jax.ShapeDtypeStruct((ALL_ROWS, 2...  146 us
    all_to_all x1, blocking collectives, on_device(): lax.all_to_all(attended.reshape(BLOCKS, ROWS, 2 * hs), 'z', 0, 0, tiled=F...  25.8 us
    pallas_call x1, Pallas kernels, prefix_part(): pl.pallas_call(prefix_kernel, out_shape=(jax.ShapeDtypeStruct((2, ALL_ROW...  18 us
    all_to_all x1, waiting for transfers between devices, on_device(): lax.all_to_all(mine, 'z', 0, 0, tiled=False).reshape(ALL_ROWS, 4 * hs)  14.9 us
    ppermute x3, waiting for transfers between devices, swapped(): return lax.ppermute(array, axis, [(0, 1), (1, 0)])  10.7 us
    all_to_all x1, starting transfers between devices, on_device(): lax.all_to_all(mine, 'z', 0, 0, tiled=False).reshape(ALL_ROWS, 4 * hs)  8.47 us
    ppermute x3, waiting for transfers between devices, on_device(): lax.ppermute(part, 'x', [(i, (i + shift) % 4) for i in range(4)])  6.41 us
    ppermute x3, starting transfers between devices, on_device(): lax.ppermute(part, 'x', [(i, (i + shift) % 4) for i in range(4)])  5.13 us
  transfers between devices with their start and end apart: 7, of which 5 were waited for; matrix products, arithmetic and copies ran while one was open for 0% of the time, Pallas kernels for 7%

profile of v1, /device:TPU:16, one launch (start us, length us, event | category | flops | bytes accessed | tf_op | source)
XLA Modules:
  0.0 244.5 jit_solution(15865286406574688176)
XLA Ops:
  0.0 1.1 copy-done
  1.1 1.0 copy-done.1
  2.1 1.0 copy-done.2
  3.1 1.4 shard_map.64
  4.5 8.5 %all-to-all-start = ((bf16[8,192,512]{2,1,0:T(8,128)(2,1)}), bf16[8,192,512]{2,1,0:T(8,128)(2,1)S(1)}, u32[]{:S(2)}, u32[]{:S(2)}) async-start(bf16[8,192,512]{2,1,0:T(8,128)(2,1)} %shard_map.64), calls=%async_computation | async-start | bytes 3145728 | tf_op jit(solution)/shard_map/all_to_all | solution.py:241
  13.0 0.9 constant_dynamic-slice_fusion
  13.9 2.8 %collective-permute-start.2 = (bf16[256,256]{1,0:T(8,128)(2,1)S(1)}, bf16[256,256]{1,0:T(8,128)(2,1)S(1)}, u32[]{:S(2)}, u32[]{:S(2)}) collective-permute-start(bf16[256,256]{1,0:T(8,128)(2,1)S(1)} %get-tuple-element.9), channel_id=1, source_target_pairs={{0,192},{64,0},{128,64},{192,128},{1,193},{65,1},{129,65},{193,129... | collective-permute-start | bytes 393224 | tf_op jit(solution)/shard_map/ppermute | solution.py:253
  16.7 0.0 collective-permute-start.1
  16.7 2.3 collective-permute-start.3
  19.0 0.2 collective-permute-done.2
  19.2 6.2 %collective-permute-done.1 = bf16[256,256]{1,0:T(8,128)(2,1)S(1)} collective-permute-done((bf16[256,256]{1,0:T(8,128)(2,1)S(1)}, bf16[256,256]{1,0:T(8,128)(2,1)S(1)}, u32[]{:S(2)}, u32[]{:S(2)}) %collective-permute-start.1) | collective-permute-done | bytes 131104 | tf_op jit(solution)/shard_map/ppermute | solution.py:253
  25.4 1.4 collective-permute-start.4
  26.9 10.2 %collective-permute-done.4 = bf16[1024,256]{1,0:T(8,128)(2,1)S(1)} collective-permute-done((bf16[1024,256]{1,0:T(8,128)(2,1)S(1)}, bf16[1024,256]{1,0:T(8,128)(2,1)S(1)}, u32[]{:S(2)}, u32[]{:S(2)}) %collective-permute-start.4) | collective-permute-done | bytes 524320 | tf_op jit(solution)/shard_map/ppermute | solution.py:232
  37.1 0.1 collective-permute-start.5
  37.9 0.1 pad_add_fusion.meta
  38.0 14.9 %all-to-all-done = bf16[8,192,512]{2,1,0:T(8,128)(2,1)S(1)} async-done(((bf16[8,192,512]{2,1,0:T(8,128)(2,1)}), bf16[8,192,512]{2,1,0:T(8,128)(2,1)S(1)}, u32[]{:S(2)}, u32[]{:S(2)}) %all-to-all-start) | async-done | bytes 1572896 | tf_op jit(solution)/shard_map/all_to_all | solution.py:241
  52.9 0.1 slice.4
  53.0 0.6 collective-permute-start
  53.6 0.0 collective-permute-done.5.prefix_b
  53.6 18.0 %shard_map.65 = (f32[2,1536,128]{2,1,0:T(8,128)S(1)}, f32[2,1536,256]{2,1,0:T(8,128)S(1)}) custom-call(bf16[1536,512]{1,0:T(8,128)(2,1)S(1)} %bitcast.8, bf16[2048,256]{1,0:T(8,128)(2,1)S(1)} %constant_dynamic-update-slice_fusion.prefix_a, bf16[2048,256]{1,0:T(8,128)(2,1)} %collective-permute-done.5.prefix_b), custom_call_target="tpu_custom_call" | custom-call | flops 12884901888 | bytes 8388608 | tf_op jit(solution)/shard_map/pallas_call | solution.py:171
  71.6 0.5 collective-permute-done.other
  72.0 145.6 %shard_map.66 = bf16[1536,256]{1,0:T(8,128)(2,1)S(1)} custom-call(s32[2]{0:T(128)S(1)} %pad_add_fusion.meta, bf16[1536,512]{1,0:T(8,128)(2,1)S(1)} %bitcast.9, bf16[1536,256]{1,0:T(8,128)(2,1)S(1)} %collective-permute-done.other, f32[2,1536,128]{2,1,0:T(8,128)S(1)} %get-tuple-element.7.shifts, f32[2,1536,256]{2,1,0:T(8,128)S(1)} %get-tuple-element.8.accum, ...), custom_call_target="tpu_custom_call" | custom-call | flops 4831838208 | bytes 8388608 | tf_op jit(solution)/shard_map/pallas_call | solution.py:188
  217.7 25.8 %all_to_all.10.by_head = bf16[8,192,256]{2,1,0:T(8,128)(2,1)S(1)} all-to-all(bf16[8,192,256]{2,1,0:T(8,128)(2,1)S(1)} %bitcast.10), channel_id=1, replica_groups=mesh['x'=4,'yl'=2,'core'=2,'z'=8,'yh'=2] {'z'}, dimensions={0} | all-to-all | bytes 1572864 | tf_op jit(solution)/shard_map/all_to_all | solution.py:261
  243.5 1.0 shard_map.67
  (10 shorter events, 0.1 us)
Async XLA Ops:
  0.0 1.1 copy-start
  1.1 1.0 copy-start.1
  2.1 1.0 copy-start.2
  4.5 48.4 %all-to-all-start = ((bf16[8,192,512]{2,1,0:T(8,128)(2,1)}), bf16[8,192,512]{2,1,0:T(8,128)(2,1)S(1)}, u32[]{:S(2)}, u32[]{:S(2)}) async-start(bf16[8,192,512]{2,1,0:T(8,128)(2,1)} %shard_map.64), calls=%async_computation | async-start | bytes 3145728 | tf_op jit(solution)/shard_map/all_to_all | solution.py:241
  13.9 5.4 %collective-permute-start.2 = (bf16[256,256]{1,0:T(8,128)(2,1)S(1)}, bf16[256,256]{1,0:T(8,128)(2,1)S(1)}, u32[]{:S(2)}, u32[]{:S(2)}) collective-permute-start(bf16[256,256]{1,0:T(8,128)(2,1)S(1)} %get-tuple-element.9), channel_id=1, source_target_pairs={{0,192},{64,0},{128,64},{192,128},{1,193},{65,1},{129,65},{193,129... | collective-permute-start | bytes 393224 | tf_op jit(solution)/shard_map/ppermute | solution.py:253
  16.7 8.7 %collective-permute-start.1 = (bf16[256,256]{1,0:T(8,128)(2,1)S(1)}, bf16[256,256]{1,0:T(8,128)(2,1)S(1)}, u32[]{:S(2)}, u32[]{:S(2)}) collective-permute-start(bf16[256,256]{1,0:T(8,128)(2,1)S(1)} %get-tuple-element.9), channel_id=1, source_target_pairs={{0,64},{64,128},{128,192},{192,0},{1,65},{65,129},{129,193},{193,1... | collective-permute-start | bytes 393224 | tf_op jit(solution)/shard_map/ppermute | solution.py:253
  16.7 8.7 %collective-permute-start.3 = (bf16[256,256]{1,0:T(8,128)(2,1)S(1)}, bf16[256,256]{1,0:T(8,128)(2,1)S(1)}, u32[]{:S(2)}, u32[]{:S(2)}) collective-permute-start(bf16[256,256]{1,0:T(8,128)(2,1)S(1)} %get-tuple-element.9), channel_id=1, source_target_pairs={{0,128},{64,192},{128,0},{192,64},{1,129},{65,193},{129,1},{193,65... | collective-permute-start | bytes 393224 | tf_op jit(solution)/shard_map/ppermute | solution.py:253
  25.4 11.7 %collective-permute-start.4 = (bf16[1024,256]{1,0:T(8,128)(2,1)S(1)}, bf16[1024,256]{1,0:T(8,128)(2,1)S(1)}, u32[]{:S(2)}, u32[]{:S(2)}) collective-permute-start(bf16[1024,256]{1,0:T(8,128)(2,1)S(1)} %pad_maximum_fusion), channel_id=1, source_target_pairs={{0,32},{32,0},{1,33},{33,1},{2,34},{34,2},{3,35},{35,3},{4,36},{36... | collective-permute-start | bytes 1572872 | tf_op jit(solution)/shard_map/ppermute | solution.py:232
  37.1 16.4 %collective-permute-start.5 = (bf16[2048,256]{1,0:T(8,128)(2,1)S(1)}, bf16[2048,256]{1,0:T(8,128)(2,1)}, u32[]{:S(2)}, u32[]{:S(2)}) collective-permute-start(bf16[2048,256]{1,0:T(8,128)(2,1)S(1)} %constant_dynamic-update-slice_fusion.prefix_a), channel_id=1, source_target_pairs={{0,16},{16,0},{1,17},{17,1},{2,18},{18,2},{3,19},{19,3},{4,20},{20... | collective-permute-start | bytes 3145736 | tf_op jit(solution)/shard_map/ppermute | solution.py:232
  53.0 19.1 %collective-permute-start = (bf16[1536,256]{1,0:T(8,128)(2,1)S(1)}, bf16[1536,256]{1,0:T(8,128)(2,1)S(1)}, u32[]{:S(2)}, u32[]{:S(2)}) collective-permute-start(bf16[1536,256]{1,0:T(8,128)(2,1)S(1)} %slice.4), channel_id=1, source_target_pairs={{0,1},{1,0},{2,3},{3,2},{4,5},{5,4},{6,7},{7,6},{8,9},{9,8},{10,11... | collective-permute-start | bytes 2359304 | tf_op jit(solution)/shard_map/ppermute | solution.py:232

commit v2 on v1

--- a/solution.py
+++ b/solution.py
@@ -12,14 +12,12 @@
 BLOCKS = 8
 ALL_ROWS = BLOCKS * ROWS
 PREFIX_HALF = 2048
-ROW_TILE = 384
-KEY_TILE = 512
+KEY_TILE = 256
 
 query_scale = 168.0 ** (-0.5)
 log2_e = 1.4426950408889634
 total_bound = 1e37
 hs = HEAD_SIZE
-q_lanes = slice(0, 2 * hs)
 k_lanes = slice(2 * hs, 3 * hs)
 v_lanes = slice(3 * hs, 4 * hs)
 
@@ -47,7 +45,6 @@
 
 
 def pair_of(queries):
-    queries = jnp.concatenate([queries[:, 0:hs], queries[:, hs : 2 * hs]], axis=0)
     scaled = queries.astype(jnp.float32) * (query_scale * log2_e)
     high = scaled.astype(jnp.bfloat16)
     low = (scaled - high.astype(jnp.float32)).astype(jnp.bfloat16)
@@ -57,12 +54,11 @@
 def prefix_kernel(mine, prefix_a, prefix_b, shifts, accum):
     tiles = [(p, i) for p in (prefix_a, prefix_b) for i in range(0, PREFIX_HALF, KEY_TILE)]
 
-    @pl.loop(0, ALL_ROWS // ROW_TILE)
-    def _(step):
-        rows = pl.ds(pl.multiple_of(step * ROW_TILE, ROW_TILE), ROW_TILE)
-        pair = pair_of(mine[rows, q_lanes])
+    @pl.loop(0, QUERY_PER_KV)
+    def _(member):
+        pair = pair_of(mine[:, pl.ds(pl.multiple_of(member * hs, hs), hs)])
         first = scores_of(pair, prefix_a[0:256, 0:hs])
-        shift = jnp.broadcast_to(jnp.max(first, axis=1, keepdims=True), (2 * ROW_TILE, 128))
+        shift = jnp.broadcast_to(jnp.max(first, axis=1, keepdims=True), (ALL_ROWS, 128))
         scores = scores_of(pair, prefix_a[0:KEY_TILE, 0:hs])
         total = None
         for j, (ref, start) in enumerate(tiles):
@@ -73,10 +69,8 @@
             added = summed_of(weights_of(scores, shift), ref[start : start + KEY_TILE, hs : 2 * hs])
             total = added if total is None else total + added
             scores = following
-        for member in range(QUERY_PER_KV):
-            part = slice(member * ROW_TILE, (member + 1) * ROW_TILE)
-            shifts[member, rows, :] = shift[part]
-            accum[member, rows, :] = total[part]
+        shifts[member] = shift
+        accum[member] = total
 
 
 def suffix_kernel(meta, mine, other, shifts, accum, prefix_a, prefix_b, out, peaks, again):
@@ -100,8 +94,12 @@
     def both(ref, block):
         return jnp.concatenate([ref[m, block * ROWS : (block + 1) * ROWS, :] for m in range(2)], axis=0)
 
+    def members_of(rows):
+        return jnp.concatenate([mine[rows, 0:hs], mine[rows, hs : 2 * hs]], axis=0)
+
     def suffix_scores(block):
-        return scores_of(pair_of(mine[block * ROWS : (block + 1) * ROWS, q_lanes]), keys_of(block, 0))
+        queries = members_of(slice(block * ROWS, (block + 1) * ROWS))
+        return scores_of(pair_of(queries), keys_of(block, 0))
 
     def finish(block, total):
         result = total[:, 0:hs] / total[:, hs : 2 * hs]
@@ -128,7 +126,7 @@
         @pl.loop(0, BLOCKS)
         def _(block):
             rows = pl.ds(pl.multiple_of(block * ROWS, ROWS), ROWS)
-            pair = pair_of(mine[rows, q_lanes])
+            pair = pair_of(members_of(rows))
             peaks[...] = jnp.full((2 * ROWS, 128), -1e30, jnp.float32)
             again[...] = jnp.zeros((2 * ROWS, 2 * hs), jnp.float32)
 
@@ -166,61 +164,51 @@
 in_vmem = pl.BlockSpec(memory_space=pltpu.VMEM)
 
 
-def prefix_part(mine, prefix_a, prefix_b):
-    count = 2 * ALL_ROWS * 2 * PREFIX_HALF
+def call(kernel, shapes, operands, scratch=(), scores=0, limit=24, specs=None):
     return pl.pallas_call(
-        prefix_kernel,
-        out_shape=(
-            jax.ShapeDtypeStruct((2, ALL_ROWS, 128), jnp.float32),
-            jax.ShapeDtypeStruct((2, ALL_ROWS, 2 * hs), jnp.float32),
+        kernel,
+        out_shape=shapes,
+        in_specs=specs or [in_vmem] * len(operands),
+        out_specs=jax.tree.map(lambda _: in_vmem, shapes),
+        scratch_shapes=scratch,
+        compiler_params=pltpu.CompilerParams(vmem_limit_bytes=limit << 20),
+        cost_estimate=pl.CostEstimate(
+            flops=scores * 256 * 4, bytes_accessed=4 << 20, transcendentals=scores
         ),
-        in_specs=[in_vmem] * 3,
-        out_specs=(in_vmem, in_vmem),
-        compiler_params=pltpu.CompilerParams(vmem_limit_bytes=24 << 20),
-        cost_estimate=pl.CostEstimate(
-            flops=count * 256 * 4, bytes_accessed=8 << 20, transcendentals=count
-        ),
-    )(mine, prefix_a, prefix_b)
-
-
-def suffix_part(meta, mine, other, shifts, accum, prefix_a, prefix_b):
-    count = 2 * ALL_ROWS * ALL_ROWS
-    return pl.pallas_call(
-        suffix_kernel,
-        out_shape=jax.ShapeDtypeStruct((ALL_ROWS, 2 * hs), jnp.bfloat16),
-        in_specs=[pl.BlockSpec(memory_space=pltpu.SMEM)] + [in_vmem] * 6,
-        out_specs=in_vmem,
-        scratch_shapes=[
-            pltpu.VMEM((2 * ROWS, 128), jnp.float32),
-            pltpu.VMEM((2 * ROWS, 2 * hs), jnp.float32),
-        ],
-        compiler_params=pltpu.CompilerParams(vmem_limit_bytes=28 << 20),
-        cost_estimate=pl.CostEstimate(
-            flops=count * 256 * 4, bytes_accessed=8 << 20, transcendentals=count
-        ),
-    )(meta, mine, other, shifts, accum, prefix_a, prefix_b)
-
-
-def split_kernel(queries, keys, values, out):
+    )(*operands)
+
+
+def f32(*shape):
+    return jax.ShapeDtypeStruct(shape, jnp.float32)
+
+
+def bf16(*shape):
+    return jax.ShapeDtypeStruct(shape, jnp.bfloat16)
+
+
+in_smem = pl.BlockSpec(memory_space=pltpu.SMEM)
+in_place = pl.BlockSpec(memory_space=pl.ANY)
+
+
+def split_kernel(queries, keys, values, out, sem):
+    copies = []
+
+    def copy(source, target):
+        copies.append(pltpu.make_async_copy(source, target, sem.at[len(copies)]))
+        copies[-1].start()
+
     for head in range(LOCAL_KV_HEADS):
-        out[head, :, q_lanes] = queries[:, 2 * head * hs : 2 * (head + 1) * hs]
-        out[head, :, k_lanes] = keys[:, head * hs : (head + 1) * hs]
-        out[head, :, v_lanes] = values[:, head * hs : (head + 1) * hs]
+        lanes = pl.ds(head * hs, hs)
+        copy(queries.at[:, pl.ds(2 * head * hs, 2 * hs)], out.at[head, :, pl.ds(0, 2 * hs)])
+        copy(keys.at[:, lanes], out.at[head, :, k_lanes])
+        copy(values.at[:, lanes], out.at[head, :, v_lanes])
+    for one in copies:
+        one.wait()
 
 
 def join_kernel(by_head, out):
     for head in range(LOCAL_KV_HEADS):
         out[:, 2 * head * hs : 2 * (head + 1) * hs] = by_head[head]
-
-
-def relaid(kernel, shape, *operands):
-    return pl.pallas_call(
-        kernel,
-        out_shape=jax.ShapeDtypeStruct(shape, jnp.bfloat16),
-        in_specs=[in_vmem] * len(operands),
-        out_specs=in_vmem,
-        compiler_params=pltpu.CompilerParams(vmem_limit_bytes=12 << 20),
-    )(*operands)
 
 
 def on_device(queries, suffix_keys, suffix_values, prefix_keys, prefix_values, lengths):
@@ -231,12 +219,13 @@
     def swapped(array, axis):
         return lax.ppermute(array, axis, [(0, 1), (1, 0)])
 
-    mine = relaid(
+    mine = call(
         split_kernel,
-        (LOCAL_KV_HEADS, ROWS, 4 * hs),
-        queries[0],
-        suffix_keys[0],
-        suffix_values[0],
+        bf16(LOCAL_KV_HEADS, ROWS, 4 * hs),
+        (queries[0], suffix_keys[0], suffix_values[0]),
+        scratch=[pltpu.SemaphoreType.DMA((3 * LOCAL_KV_HEADS,))],
+        limit=60,
+        specs=[in_place] * 3,
     )
     mine = lax.all_to_all(mine, "z", 0, 0, tiled=False).reshape(ALL_ROWS, 4 * hs)
     other = swapped(mine[:, 2 * hs :], "yh")
@@ -256,10 +245,23 @@
     prefix_a = jnp.concatenate([column, swapped(column, "yl")], axis=0)
     prefix_b = swapped(prefix_a, "core")
 
-    shifts, accum = prefix_part(mine, prefix_a, prefix_b)
-    attended = suffix_part(meta, mine, other, shifts, accum, prefix_a, prefix_b)
+    state = call(
+        prefix_kernel,
+        (f32(2, ALL_ROWS, 128), f32(2, ALL_ROWS, 2 * hs)),
+        (mine, prefix_a, prefix_b),
+        scores=4 * ALL_ROWS * PREFIX_HALF,
+    )
+    attended = call(
+        suffix_kernel,
+        bf16(ALL_ROWS, 2 * hs),
+        (meta, mine, other, *state, prefix_a, prefix_b),
+        scratch=[pltpu.VMEM((2 * ROWS, 128), jnp.float32), pltpu.VMEM((2 * ROWS, 2 * hs), jnp.float32)],
+        scores=2 * ALL_ROWS * ALL_ROWS,
+        limit=28,
+        specs=[in_smem] + [in_vmem] * 6,
+    )
     attended = lax.all_to_all(attended.reshape(BLOCKS, ROWS, 2 * hs), "z", 0, 0, tiled=False)
-    return relaid(join_kernel, (ROWS, LOCAL_KV_HEADS * 2 * hs), attended)[None]
+    return call(join_kernel, bf16(ROWS, LOCAL_KV_HEADS * 2 * hs), (attended,), limit=12)[None]
 
 
 def solution(mesh):

time: 246 us -> 243 us (0.988)
  local copies, waits for them, and re-layouts: 4.12 us -> 1 us
    unnamed x9 -> x3, local copies, waits for them, and re-layouts: 3.15 us -> 0.03 us
where the time goes in v2:
time: 243 us
  Pallas kernels  165 us (68%)
  waiting for transfers between devices  34 us (14%)
  blocking collectives  25.9 us (11%)
  starting transfers between devices  15.5 us (6%)
    pallas_call x4, Pallas kernels, call(): pl.pallas_call(kernel, out_shape=shapes, in_specs=specs or [in_vmem] * le...  165 us
    all_to_all x1, blocking collectives, on_device(): lax.all_to_all(attended.reshape(BLOCKS, ROWS, 2 * hs), 'z', 0, 0, tiled=F...  25.9 us
    all_to_all x1, waiting for transfers between devices, on_device(): lax.all_to_all(mine, 'z', 0, 0, tiled=False).reshape(ALL_ROWS, 4 * hs)  14.9 us
    ppermute x3, waiting for transfers between devices, swapped(): return lax.ppermute(array, axis, [(0, 1), (1, 0)])  12.7 us
    all_to_all x1, starting transfers between devices, on_device(): lax.all_to_all(mine, 'z', 0, 0, tiled=False).reshape(ALL_ROWS, 4 * hs)  8.48 us
    ppermute x3, waiting for transfers between devices, on_device(): lax.ppermute(part, 'x', [(i, (i + shift) % 4) for i in range(4)])  6.41 us
    ppermute x3, starting transfers between devices, on_device(): lax.ppermute(part, 'x', [(i, (i + shift) % 4) for i in range(4)])  5.13 us
  transfers between devices with their start and end apart: 7, of which 5 were waited for; matrix products, arithmetic and copies ran while one was open for 0% of the time, Pallas kernels for 7%

profile of v2, /device:TPU:16, one launch (start us, length us, event | category | flops | bytes accessed | tf_op | source)
XLA Modules:
  0.0 242.6 jit_solution(17217571878087665424)
XLA Ops:
  0.0 2.8 %shard_map.64 = bf16[8,192,512]{2,1,0:T(8,128)(2,1)} custom-call(bf16[192,2048]{1,0:T(8,128)(2,1)} %bitcast.11, bf16[192,1024]{1,0:T(8,128)(2,1)} %bitcast.12, bf16[192,1024]{1,0:T(8,128)(2,1)} %bitcast.13), custom_call_target="tpu_custom_call" | custom-call | bytes 4194304 | tf_op jit(solution)/shard_map/pallas_call | solution.py:168
  2.8 8.5 %all-to-all-start = ((bf16[8,192,512]{2,1,0:T(8,128)(2,1)}), bf16[8,192,512]{2,1,0:T(8,128)(2,1)S(1)}, u32[]{:S(2)}, u32[]{:S(2)}) async-start(bf16[8,192,512]{2,1,0:T(8,128)(2,1)} %shard_map.64), calls=%async_computation | async-start | bytes 3145728 | tf_op jit(solution)/shard_map/all_to_all | solution.py:230
  11.3 0.9 constant_dynamic-slice_fusion
  12.2 2.8 %collective-permute-start.2 = (bf16[256,256]{1,0:T(8,128)(2,1)S(1)}, bf16[256,256]{1,0:T(8,128)(2,1)S(1)}, u32[]{:S(2)}, u32[]{:S(2)}) collective-permute-start(bf16[256,256]{1,0:T(8,128)(2,1)S(1)} %get-tuple-element.9), channel_id=1, source_target_pairs={{0,192},{64,0},{128,64},{192,128},{1,193},{65,1},{129,65},{193,129... | collective-permute-start | bytes 393224 | tf_op jit(solution)/shard_map/ppermute | solution.py:242
  15.1 0.0 collective-permute-start.1
  15.1 2.3 collective-permute-start.3
  17.3 0.2 collective-permute-done.2
  17.6 6.2 %collective-permute-done.1 = bf16[256,256]{1,0:T(8,128)(2,1)S(1)} collective-permute-done((bf16[256,256]{1,0:T(8,128)(2,1)S(1)}, bf16[256,256]{1,0:T(8,128)(2,1)S(1)}, u32[]{:S(2)}, u32[]{:S(2)}) %collective-permute-start.1) | collective-permute-done | bytes 131104 | tf_op jit(solution)/shard_map/ppermute | solution.py:242
  23.8 0.0 collective-permute-done.3
  23.8 1.4 collective-permute-start.4
  25.2 10.2 %collective-permute-done.4 = bf16[1024,256]{1,0:T(8,128)(2,1)S(1)} collective-permute-done((bf16[1024,256]{1,0:T(8,128)(2,1)S(1)}, bf16[1024,256]{1,0:T(8,128)(2,1)S(1)}, u32[]{:S(2)}, u32[]{:S(2)}) %collective-permute-start.4) | collective-permute-done | bytes 524320 | tf_op jit(solution)/shard_map/ppermute | solution.py:220
  35.5 0.1 collective-permute-start.5
  36.3 0.1 pad_add_fusion.meta
  36.3 14.9 %all-to-all-done = bf16[8,192,512]{2,1,0:T(8,128)(2,1)S(1)} async-done(((bf16[8,192,512]{2,1,0:T(8,128)(2,1)}), bf16[8,192,512]{2,1,0:T(8,128)(2,1)S(1)}, u32[]{:S(2)}, u32[]{:S(2)}) %all-to-all-start) | async-done | bytes 1572896 | tf_op jit(solution)/shard_map/all_to_all | solution.py:230
  51.3 0.1 slice.4
  51.3 0.4 collective-permute-start
  51.8 0.0 collective-permute-done.5.prefix_b
  51.8 16.0 %shard_map.65 = (f32[2,1536,128]{2,1,0:T(8,128)S(1)}, f32[2,1536,256]{2,1,0:T(8,128)S(1)}) custom-call(bf16[1536,512]{1,0:T(8,128)(2,1)S(1)} %bitcast.8, bf16[2048,256]{1,0:T(8,128)(2,1)S(1)} %constant_dynamic-update-slice_fusion.prefix_a, bf16[2048,256]{1,0:T(8,128)(2,1)} %collective-permute-done.5.prefix_b), custom_call_target="tpu_custom_call" | custom-call | flops 12884901888 | bytes 4194304 | tf_op jit(solution)/shard_map/pallas_call | solution.py:168
  67.8 2.4 %collective-permute-done.other = bf16[1536,256]{1,0:T(8,128)(2,1)S(1)} collective-permute-done((bf16[1536,256]{1,0:T(8,128)(2,1)S(1)}, bf16[1536,256]{1,0:T(8,128)(2,1)S(1)}, u32[]{:S(2)}, u32[]{:S(2)}) %collective-permute-start) | collective-permute-done | bytes 786464 | tf_op jit(solution)/shard_map/ppermute | solution.py:220
  70.2 145.5 %shard_map.66 = bf16[1536,256]{1,0:T(8,128)(2,1)S(1)} custom-call(s32[2]{0:T(128)S(1)} %pad_add_fusion.meta, bf16[1536,512]{1,0:T(8,128)(2,1)S(1)} %bitcast.9, bf16[1536,256]{1,0:T(8,128)(2,1)S(1)} %collective-permute-done.other, f32[2,1536,128]{2,1,0:T(8,128)S(1)} %get-tuple-element.7.shifts, f32[2,1536,256]{2,1,0:T(8,128)S(1)} %get-tuple-element.8.accum, ...), custom_call_target="tpu_custom_call" | custom-call | flops 4831838208 | bytes 4194304 | tf_op jit(solution)/shard_map/pallas_call | solution.py:168
  215.8 25.9 %all_to_all.10.by_head = bf16[8,192,256]{2,1,0:T(8,128)(2,1)S(1)} all-to-all(bf16[8,192,256]{2,1,0:T(8,128)(2,1)S(1)} %bitcast.10), channel_id=1, replica_groups=mesh['x'=4,'yl'=2,'core'=2,'z'=8,'yh'=2] {'z'}, dimensions={0} | all-to-all | bytes 1572864 | tf_op jit(solution)/shard_map/all_to_all | solution.py:263
  241.6 1.0 shard_map.67
  (6 shorter events, 0.1 us)
Async XLA Ops:
  2.8 48.4 %all-to-all-start = ((bf16[8,192,512]{2,1,0:T(8,128)(2,1)}), bf16[8,192,512]{2,1,0:T(8,128)(2,1)S(1)}, u32[]{:S(2)}, u32[]{:S(2)}) async-start(bf16[8,192,512]{2,1,0:T(8,128)(2,1)} %shard_map.64), calls=%async_computation | async-start | bytes 3145728 | tf_op jit(solution)/shard_map/all_to_all | solution.py:230
  12.2 5.4 %collective-permute-start.2 = (bf16[256,256]{1,0:T(8,128)(2,1)S(1)}, bf16[256,256]{1,0:T(8,128)(2,1)S(1)}, u32[]{:S(2)}, u32[]{:S(2)}) collective-permute-start(bf16[256,256]{1,0:T(8,128)(2,1)S(1)} %get-tuple-element.9), channel_id=1, source_target_pairs={{0,192},{64,0},{128,64},{192,128},{1,193},{65,1},{129,65},{193,129... | collective-permute-start | bytes 393224 | tf_op jit(solution)/shard_map/ppermute | solution.py:242
  15.1 8.7 %collective-permute-start.1 = (bf16[256,256]{1,0:T(8,128)(2,1)S(1)}, bf16[256,256]{1,0:T(8,128)(2,1)S(1)}, u32[]{:S(2)}, u32[]{:S(2)}) collective-permute-start(bf16[256,256]{1,0:T(8,128)(2,1)S(1)} %get-tuple-element.9), channel_id=1, source_target_pairs={{0,64},{64,128},{128,192},{192,0},{1,65},{65,129},{129,193},{193,1... | collective-permute-start | bytes 393224 | tf_op jit(solution)/shard_map/ppermute | solution.py:242
  15.1 8.7 %collective-permute-start.3 = (bf16[256,256]{1,0:T(8,128)(2,1)S(1)}, bf16[256,256]{1,0:T(8,128)(2,1)S(1)}, u32[]{:S(2)}, u32[]{:S(2)}) collective-permute-start(bf16[256,256]{1,0:T(8,128)(2,1)S(1)} %get-tuple-element.9), channel_id=1, source_target_pairs={{0,128},{64,192},{128,0},{192,64},{1,129},{65,193},{129,1},{193,65... | collective-permute-start | bytes 393224 | tf_op jit(solution)/shard_map/ppermute | solution.py:242
  23.8 11.7 %collective-permute-start.4 = (bf16[1024,256]{1,0:T(8,128)(2,1)S(1)}, bf16[1024,256]{1,0:T(8,128)(2,1)S(1)}, u32[]{:S(2)}, u32[]{:S(2)}) collective-permute-start(bf16[1024,256]{1,0:T(8,128)(2,1)S(1)} %pad_maximum_fusion), channel_id=1, source_target_pairs={{0,32},{32,0},{1,33},{33,1},{2,34},{34,2},{3,35},{35,3},{4,36},{36... | collective-permute-start | bytes 1572872 | tf_op jit(solution)/shard_map/ppermute | solution.py:220
  35.5 16.2 %collective-permute-start.5 = (bf16[2048,256]{1,0:T(8,128)(2,1)S(1)}, bf16[2048,256]{1,0:T(8,128)(2,1)}, u32[]{:S(2)}, u32[]{:S(2)}) collective-permute-start(bf16[2048,256]{1,0:T(8,128)(2,1)S(1)} %constant_dynamic-update-slice_fusion.prefix_a), channel_id=1, source_target_pairs={{0,16},{16,0},{1,17},{17,1},{2,18},{18,2},{3,19},{19,3},{4,20},{20... | collective-permute-start | bytes 3145736 | tf_op jit(solution)/shard_map/ppermute | solution.py:220
  51.3 18.9 %collective-permute-start = (bf16[1536,256]{1,0:T(8,128)(2,1)S(1)}, bf16[1536,256]{1,0:T(8,128)(2,1)S(1)}, u32[]{:S(2)}, u32[]{:S(2)}) collective-permute-start(bf16[1536,256]{1,0:T(8,128)(2,1)S(1)} %slice.4), channel_id=1, source_target_pairs={{0,1},{1,0},{2,3},{3,2},{4,5},{5,4},{6,7},{7,6},{8,9},{9,8},{10,11... | collective-permute-start | bytes 2359304 | tf_op jit(solution)/shard_map/ppermute | solution.py:220

commit v3 on v2

--- a/solution.py
+++ b/solution.py
@@ -59,21 +59,19 @@
         pair = pair_of(mine[:, pl.ds(pl.multiple_of(member * hs, hs), hs)])
         first = scores_of(pair, prefix_a[0:256, 0:hs])
         shift = jnp.broadcast_to(jnp.max(first, axis=1, keepdims=True), (ALL_ROWS, 128))
+        shifts[member] = shift
         scores = scores_of(pair, prefix_a[0:KEY_TILE, 0:hs])
-        total = None
         for j, (ref, start) in enumerate(tiles):
             following = None
             if j + 1 < len(tiles):
                 next_ref, next_start = tiles[j + 1]
                 following = scores_of(pair, next_ref[next_start : next_start + KEY_TILE, 0:hs])
             added = summed_of(weights_of(scores, shift), ref[start : start + KEY_TILE, hs : 2 * hs])
-            total = added if total is None else total + added
+            accum[member] = added if j == 0 else accum[member] + added
             scores = following
-        shifts[member] = shift
-        accum[member] = total
-
-
-def suffix_kernel(meta, mine, other, shifts, accum, prefix_a, prefix_b, out, peaks, again):
+
+
+def suffix_kernel(meta, mine, other, shifts, accum, prefix_a, prefix_b, out, peaks, again, held):
     second = meta[0]
     length = meta[1]
     row_ids = lax.broadcasted_iota(jnp.int32, (2 * ROWS, 2 * ROWS), 0)
@@ -123,6 +121,8 @@
 
     @pl.when(jnp.max(beyond) > 0.0)
     def _():
+        pltpu.sync_copy(prefix_b, held)
+
         @pl.loop(0, BLOCKS)
         def _(block):
             rows = pl.ds(pl.multiple_of(block * ROWS, ROWS), ROWS)
@@ -140,7 +140,7 @@
                 again[...] = again[...] * jnp.exp2(old - new) + summed_of(weights, values)
                 peaks[...] = jnp.broadcast_to(new, (2 * ROWS, 128))
 
-            for ref in (prefix_a, prefix_b):
+            for ref in (prefix_a, held):
 
                 @pl.loop(0, PREFIX_HALF // 256)
                 def _(i):
@@ -164,12 +164,12 @@
 in_vmem = pl.BlockSpec(memory_space=pltpu.VMEM)
 
 
-def call(kernel, shapes, operands, scratch=(), scores=0, limit=24, specs=None):
+def call(kernel, shapes, operands, scratch=(), scores=0, limit=24, specs=None, outs=None):
     return pl.pallas_call(
         kernel,
         out_shape=shapes,
         in_specs=specs or [in_vmem] * len(operands),
-        out_specs=jax.tree.map(lambda _: in_vmem, shapes),
+        out_specs=outs or jax.tree.map(lambda _: in_vmem, shapes),
         scratch_shapes=scratch,
         compiler_params=pltpu.CompilerParams(vmem_limit_bytes=limit << 20),
         cost_estimate=pl.CostEstimate(
@@ -190,20 +190,30 @@
 in_place = pl.BlockSpec(memory_space=pl.ANY)
 
 
-def split_kernel(queries, keys, values, out, sem):
-    copies = []
-
-    def copy(source, target):
-        copies.append(pltpu.make_async_copy(source, target, sem.at[len(copies)]))
-        copies[-1].start()
-
+def split_kernel(queries, keys, values, out, held, arrived, left):
+    arriving, leaving = [], []
     for head in range(LOCAL_KV_HEADS):
         lanes = pl.ds(head * hs, hs)
-        copy(queries.at[:, pl.ds(2 * head * hs, 2 * hs)], out.at[head, :, pl.ds(0, 2 * hs)])
-        copy(keys.at[:, lanes], out.at[head, :, k_lanes])
-        copy(values.at[:, lanes], out.at[head, :, v_lanes])
-    for one in copies:
-        one.wait()
+        parts = (
+            (queries.at[:, pl.ds(2 * head * hs, 2 * hs)], pl.ds(0, 2 * hs)),
+            (keys.at[:, lanes], pl.ds(2 * hs, hs)),
+            (values.at[:, lanes], pl.ds(3 * hs, hs)),
+        )
+        arriving.append(
+            [
+                pltpu.make_async_copy(source, held.at[head, :, target], arrived.at[head, i])
+                for i, (source, target) in enumerate(parts)
+            ]
+        )
+        for copy in arriving[-1]:
+            copy.start()
+    for head in range(LOCAL_KV_HEADS):
+        for copy in arriving[head]:
+            copy.wait()
+        leaving.append(pltpu.make_async_copy(held.at[head], out.at[head], left.at[head]))
+        leaving[-1].start()
+    for copy in leaving:
+        copy.wait()
 
 
 def join_kernel(by_head, out):
@@ -223,9 +233,14 @@
         split_kernel,
         bf16(LOCAL_KV_HEADS, ROWS, 4 * hs),
         (queries[0], suffix_keys[0], suffix_values[0]),
-        scratch=[pltpu.SemaphoreType.DMA((3 * LOCAL_KV_HEADS,))],
+        scratch=[
+            pltpu.VMEM((LOCAL_KV_HEADS, ROWS, 4 * hs), jnp.bfloat16),
+            pltpu.SemaphoreType.DMA((LOCAL_KV_HEADS, 3)),
+            pltpu.SemaphoreType.DMA((LOCAL_KV_HEADS,)),
+        ],
         limit=60,
         specs=[in_place] * 3,
+        outs=in_place,
     )
     mine = lax.all_to_all(mine, "z", 0, 0, tiled=False).reshape(ALL_ROWS, 4 * hs)
     other = swapped(mine[:, 2 * hs :], "yh")
@@ -255,10 +270,10 @@
         suffix_kernel,
         bf16(ALL_ROWS, 2 * hs),
         (meta, mine, other, *state, prefix_a, prefix_b),
-        scratch=[pltpu.VMEM((2 * ROWS, 128), jnp.float32), pltpu.VMEM((2 * ROWS, 2 * hs), jnp.float32)],
+        scratch=[pltpu.VMEM((2 * ROWS, 128), jnp.float32), pltpu.VMEM((2 * ROWS, 2 * hs), jnp.float32), pltpu.VMEM((PREFIX_HALF, 2 * hs), jnp.bfloat16)],
         scores=2 * ALL_ROWS * ALL_ROWS,
         limit=28,
-        specs=[in_smem] + [in_vmem] * 6,
+        specs=[in_smem] + [in_vmem] * 5 + [in_place],
     )
     attended = lax.all_to_all(attended.reshape(BLOCKS, ROWS, 2 * hs), "z", 0, 0, tiled=False)
     return call(join_kernel, bf16(ROWS, LOCAL_KV_HEADS * 2 * hs), (attended,), limit=12)[None]

time: 243 us -> 243 us (level)
  no operation moved by 1% of the time
where the time goes in v3:
time: 243 us
  Pallas kernels  165 us (68%)
  waiting for transfers between devices  34.1 us (14%)
  blocking collectives  25.9 us (11%)
  starting transfers between devices  15.5 us (6%)
    pallas_call x4, Pallas kernels, call(): pl.pallas_call(kernel, out_shape=shapes, in_specs=specs or [in_vmem] * le...  165 us
    all_to_all x1, blocking collectives, on_device(): lax.all_to_all(attended.reshape(BLOCKS, ROWS, 2 * hs), 'z', 0, 0, tiled=F...  25.9 us
    all_to_all x1, waiting for transfers between devices, on_device(): lax.all_to_all(mine, 'z', 0, 0, tiled=False).reshape(ALL_ROWS, 4 * hs)  14.9 us
    ppermute x3, waiting for transfers between devices, swapped(): return lax.ppermute(array, axis, [(0, 1), (1, 0)])  12.7 us
    all_to_all x1, starting transfers between devices, on_device(): lax.all_to_all(mine, 'z', 0, 0, tiled=False).reshape(ALL_ROWS, 4 * hs)  8.48 us
    ppermute x3, waiting for transfers between devices, on_device(): lax.ppermute(part, 'x', [(i, (i + shift) % 4) for i in range(4)])  6.41 us
    ppermute x3, starting transfers between devices, on_device(): lax.ppermute(part, 'x', [(i, (i + shift) % 4) for i in range(4)])  5.13 us
  transfers between devices with their start and end apart: 7, of which 5 were waited for; matrix products, arithmetic and copies ran while one was open for 0% of the time, Pallas kernels for 7%

profile of v3, /device:TPU:16, one launch (start us, length us, event | category | flops | bytes accessed | tf_op | source)
XLA Modules:
  0.0 242.8 jit_solution(11754790048992223894)
XLA Ops:
  0.0 2.5 %shard_map.64 = bf16[8,192,512]{2,1,0:T(8,128)(2,1)} custom-call(bf16[192,2048]{1,0:T(8,128)(2,1)} %bitcast.11, bf16[192,1024]{1,0:T(8,128)(2,1)} %bitcast.12, bf16[192,1024]{1,0:T(8,128)(2,1)} %bitcast.13), custom_call_target="tpu_custom_call" | custom-call | bytes 4194304 | tf_op jit(solution)/shard_map/pallas_call | solution.py:168
  2.5 8.5 %all-to-all-start = ((bf16[8,192,512]{2,1,0:T(8,128)(2,1)}), bf16[8,192,512]{2,1,0:T(8,128)(2,1)S(1)}, u32[]{:S(2)}, u32[]{:S(2)}) async-start(bf16[8,192,512]{2,1,0:T(8,128)(2,1)} %shard_map.64), calls=%async_computation | async-start | bytes 3145728 | tf_op jit(solution)/shard_map/all_to_all | solution.py:245
  10.9 0.9 constant_dynamic-slice_fusion
  11.9 2.8 %collective-permute-start.2 = (bf16[256,256]{1,0:T(8,128)(2,1)S(1)}, bf16[256,256]{1,0:T(8,128)(2,1)S(1)}, u32[]{:S(2)}, u32[]{:S(2)}) collective-permute-start(bf16[256,256]{1,0:T(8,128)(2,1)S(1)} %get-tuple-element.9), channel_id=1, source_target_pairs={{0,192},{64,0},{128,64},{192,128},{1,193},{65,1},{129,65},{193,129... | collective-permute-start | bytes 393224 | tf_op jit(solution)/shard_map/ppermute | solution.py:257
  14.7 0.0 collective-permute-start.1
  14.7 2.3 collective-permute-start.3
  17.0 0.2 collective-permute-done.2
  17.2 6.2 %collective-permute-done.1 = bf16[256,256]{1,0:T(8,128)(2,1)S(1)} collective-permute-done((bf16[256,256]{1,0:T(8,128)(2,1)S(1)}, bf16[256,256]{1,0:T(8,128)(2,1)S(1)}, u32[]{:S(2)}, u32[]{:S(2)}) %collective-permute-start.1) | collective-permute-done | bytes 131104 | tf_op jit(solution)/shard_map/ppermute | solution.py:257
  23.4 0.0 collective-permute-done.3
  23.4 1.4 collective-permute-start.4
  24.9 10.2 %collective-permute-done.4 = bf16[1024,256]{1,0:T(8,128)(2,1)S(1)} collective-permute-done((bf16[1024,256]{1,0:T(8,128)(2,1)S(1)}, bf16[1024,256]{1,0:T(8,128)(2,1)S(1)}, u32[]{:S(2)}, u32[]{:S(2)}) %collective-permute-start.4) | collective-permute-done | bytes 524320 | tf_op jit(solution)/shard_map/ppermute | solution.py:230
  35.1 0.1 collective-permute-start.5
  35.9 0.1 pad_add_fusion.meta
  36.0 14.9 %all-to-all-done = bf16[8,192,512]{2,1,0:T(8,128)(2,1)S(1)} async-done(((bf16[8,192,512]{2,1,0:T(8,128)(2,1)}), bf16[8,192,512]{2,1,0:T(8,128)(2,1)S(1)}, u32[]{:S(2)}, u32[]{:S(2)}) %all-to-all-start) | async-done | bytes 1572896 | tf_op jit(solution)/shard_map/all_to_all | solution.py:245
  50.9 0.1 slice.4
  51.0 0.4 collective-permute-start
  51.4 0.0 collective-permute-done.5.prefix_b
  51.4 16.0 %shard_map.65 = (f32[2,1536,128]{2,1,0:T(8,128)S(1)}, f32[2,1536,256]{2,1,0:T(8,128)S(1)}) custom-call(bf16[1536,512]{1,0:T(8,128)(2,1)S(1)} %bitcast.8, bf16[2048,256]{1,0:T(8,128)(2,1)S(1)} %constant_dynamic-update-slice_fusion.prefix_a, bf16[2048,256]{1,0:T(8,128)(2,1)} %collective-permute-done.5.prefix_b), custom_call_target="tpu_custom_call" | custom-call | flops 12884901888 | bytes 4194304 | tf_op jit(solution)/shard_map/pallas_call | solution.py:168
  67.4 2.5 %collective-permute-done.other = bf16[1536,256]{1,0:T(8,128)(2,1)S(1)} collective-permute-done((bf16[1536,256]{1,0:T(8,128)(2,1)S(1)}, bf16[1536,256]{1,0:T(8,128)(2,1)S(1)}, u32[]{:S(2)}, u32[]{:S(2)}) %collective-permute-start) | collective-permute-done | bytes 786464 | tf_op jit(solution)/shard_map/ppermute | solution.py:230
  69.9 146.1 %shard_map.66 = bf16[1536,256]{1,0:T(8,128)(2,1)S(1)} custom-call(s32[2]{0:T(128)S(1)} %pad_add_fusion.meta, bf16[1536,512]{1,0:T(8,128)(2,1)S(1)} %bitcast.9, bf16[1536,256]{1,0:T(8,128)(2,1)S(1)} %collective-permute-done.other, f32[2,1536,128]{2,1,0:T(8,128)S(1)} %get-tuple-element.7.shifts, f32[2,1536,256]{2,1,0:T(8,128)S(1)} %get-tuple-element.8.accum, ...), custom_call_target="tpu_custom_call" | custom-call | flops 4831838208 | bytes 4194304 | tf_op jit(solution)/shard_map/pallas_call | solution.py:168
  215.9 25.9 %all_to_all.10.by_head = bf16[8,192,256]{2,1,0:T(8,128)(2,1)S(1)} all-to-all(bf16[8,192,256]{2,1,0:T(8,128)(2,1)S(1)} %bitcast.10), channel_id=1, replica_groups=mesh['x'=4,'yl'=2,'core'=2,'z'=8,'yh'=2] {'z'}, dimensions={0} | all-to-all | bytes 1572864 | tf_op jit(solution)/shard_map/all_to_all | solution.py:278
  241.8 1.0 shard_map.67
  (6 shorter events, 0.1 us)
Async XLA Ops:
  2.5 48.4 %all-to-all-start = ((bf16[8,192,512]{2,1,0:T(8,128)(2,1)}), bf16[8,192,512]{2,1,0:T(8,128)(2,1)S(1)}, u32[]{:S(2)}, u32[]{:S(2)}) async-start(bf16[8,192,512]{2,1,0:T(8,128)(2,1)} %shard_map.64), calls=%async_computation | async-start | bytes 3145728 | tf_op jit(solution)/shard_map/all_to_all | solution.py:245
  11.9 5.4 %collective-permute-start.2 = (bf16[256,256]{1,0:T(8,128)(2,1)S(1)}, bf16[256,256]{1,0:T(8,128)(2,1)S(1)}, u32[]{:S(2)}, u32[]{:S(2)}) collective-permute-start(bf16[256,256]{1,0:T(8,128)(2,1)S(1)} %get-tuple-element.9), channel_id=1, source_target_pairs={{0,192},{64,0},{128,64},{192,128},{1,193},{65,1},{129,65},{193,129... | collective-permute-start | bytes 393224 | tf_op jit(solution)/shard_map/ppermute | solution.py:257
  14.7 8.7 %collective-permute-start.1 = (bf16[256,256]{1,0:T(8,128)(2,1)S(1)}, bf16[256,256]{1,0:T(8,128)(2,1)S(1)}, u32[]{:S(2)}, u32[]{:S(2)}) collective-permute-start(bf16[256,256]{1,0:T(8,128)(2,1)S(1)} %get-tuple-element.9), channel_id=1, source_target_pairs={{0,64},{64,128},{128,192},{192,0},{1,65},{65,129},{129,193},{193,1... | collective-permute-start | bytes 393224 | tf_op jit(solution)/shard_map/ppermute | solution.py:257
  14.7 8.7 %collective-permute-start.3 = (bf16[256,256]{1,0:T(8,128)(2,1)S(1)}, bf16[256,256]{1,0:T(8,128)(2,1)S(1)}, u32[]{:S(2)}, u32[]{:S(2)}) collective-permute-start(bf16[256,256]{1,0:T(8,128)(2,1)S(1)} %get-tuple-element.9), channel_id=1, source_target_pairs={{0,128},{64,192},{128,0},{192,64},{1,129},{65,193},{129,1},{193,65... | collective-permute-start | bytes 393224 | tf_op jit(solution)/shard_map/ppermute | solution.py:257
  23.4 11.7 %collective-permute-start.4 = (bf16[1024,256]{1,0:T(8,128)(2,1)S(1)}, bf16[1024,256]{1,0:T(8,128)(2,1)S(1)}, u32[]{:S(2)}, u32[]{:S(2)}) collective-permute-start(bf16[1024,256]{1,0:T(8,128)(2,1)S(1)} %pad_maximum_fusion), channel_id=1, source_target_pairs={{0,32},{32,0},{1,33},{33,1},{2,34},{34,2},{3,35},{35,3},{4,36},{36... | collective-permute-start | bytes 1572872 | tf_op jit(solution)/shard_map/ppermute | solution.py:230
  35.1 16.2 %collective-permute-start.5 = (bf16[2048,256]{1,0:T(8,128)(2,1)S(1)}, bf16[2048,256]{1,0:T(8,128)(2,1)}, u32[]{:S(2)}, u32[]{:S(2)}) collective-permute-start(bf16[2048,256]{1,0:T(8,128)(2,1)S(1)} %constant_dynamic-update-slice_fusion.prefix_a), channel_id=1, source_target_pairs={{0,16},{16,0},{1,17},{17,1},{2,18},{18,2},{3,19},{19,3},{4,20},{20... | collective-permute-start | bytes 3145736 | tf_op jit(solution)/shard_map/ppermute | solution.py:230
  51.0 18.9 %collective-permute-start = (bf16[1536,256]{1,0:T(8,128)(2,1)S(1)}, bf16[1536,256]{1,0:T(8,128)(2,1)S(1)}, u32[]{:S(2)}, u32[]{:S(2)}) collective-permute-start(bf16[1536,256]{1,0:T(8,128)(2,1)S(1)} %slice.4), channel_id=1, source_target_pairs={{0,1},{1,0},{2,3},{3,2},{4,5},{5,4},{6,7},{7,6},{8,9},{9,8},{10,11... | collective-permute-start | bytes 2359304 | tf_op jit(solution)/shard_map/ppermute | solution.py:230

commit v4 on v3

--- a/solution.py
+++ b/solution.py
@@ -51,8 +51,10 @@
     return jnp.concatenate([high, low], axis=1)
 
 
-def prefix_kernel(mine, prefix_a, prefix_b, shifts, accum):
-    tiles = [(p, i) for p in (prefix_a, prefix_b) for i in range(0, PREFIX_HALF, KEY_TILE)]
+def prefix_kernel(mine, prefix_a, prefix_b, shifts, accum, held, arrived):
+    arriving = pltpu.make_async_copy(prefix_b, held, arrived)
+    arriving.start()
+    tiles = [(p, i) for p in (prefix_a, held) for i in range(0, PREFIX_HALF, KEY_TILE)]
 
     @pl.loop(0, QUERY_PER_KV)
     def _(member):
@@ -60,6 +62,7 @@
         first = scores_of(pair, prefix_a[0:256, 0:hs])
         shift = jnp.broadcast_to(jnp.max(first, axis=1, keepdims=True), (ALL_ROWS, 128))
         shifts[member] = shift
+        pl.when(member == 0)(arriving.wait)
         scores = scores_of(pair, prefix_a[0:KEY_TILE, 0:hs])
         for j, (ref, start) in enumerate(tiles):
             following = None
@@ -264,6 +267,8 @@
         prefix_kernel,
         (f32(2, ALL_ROWS, 128), f32(2, ALL_ROWS, 2 * hs)),
         (mine, prefix_a, prefix_b),
+        scratch=[pltpu.VMEM((PREFIX_HALF, 2 * hs), jnp.bfloat16), pltpu.SemaphoreType.DMA],
+        specs=[in_vmem] * 2 + [in_place],
         scores=4 * ALL_ROWS * PREFIX_HALF,
     )
     attended = call(

time: 243 us -> 243 us (level)
  no operation moved by 1% of the time
where the time goes in v4:
time: 243 us
  Pallas kernels  165 us (68%)
  waiting for transfers between devices  34.1 us (14%)
  blocking collectives  25.9 us (11%)
  starting transfers between devices  15.5 us (6%)
    pallas_call x4, Pallas kernels, call(): pl.pallas_call(kernel, out_shape=shapes, in_specs=specs or [in_vmem] * le...  165 us
    all_to_all x1, blocking collectives, on_device(): lax.all_to_all(attended.reshape(BLOCKS, ROWS, 2 * hs), 'z', 0, 0, tiled=F...  25.9 us
    all_to_all x1, waiting for transfers between devices, on_device(): lax.all_to_all(mine, 'z', 0, 0, tiled=False).reshape(ALL_ROWS, 4 * hs)  14.9 us
    ppermute x3, waiting for transfers between devices, swapped(): return lax.ppermute(array, axis, [(0, 1), (1, 0)])  12.7 us
    all_to_all x1, starting transfers between devices, on_device(): lax.all_to_all(mine, 'z', 0, 0, tiled=False).reshape(ALL_ROWS, 4 * hs)  8.48 us
    ppermute x3, waiting for transfers between devices, on_device(): lax.ppermute(part, 'x', [(i, (i + shift) % 4) for i in range(4)])  6.41 us
    ppermute x3, starting transfers between devices, on_device(): lax.ppermute(part, 'x', [(i, (i + shift) % 4) for i in range(4)])  5.13 us
  transfers between devices with their start and end apart: 7, of which 5 were waited for; matrix products, arithmetic and copies ran while one was open for 0% of the time, Pallas kernels for 7%

profile of v4, /device:TPU:16, one launch (start us, length us, event | category | flops | bytes accessed | tf_op | source)
XLA Modules:
  0.0 242.8 jit_solution(16721154706429383106)
XLA Ops:
  0.0 2.5 %shard_map.64 = bf16[8,192,512]{2,1,0:T(8,128)(2,1)} custom-call(bf16[192,2048]{1,0:T(8,128)(2,1)} %bitcast.11, bf16[192,1024]{1,0:T(8,128)(2,1)} %bitcast.12, bf16[192,1024]{1,0:T(8,128)(2,1)} %bitcast.13), custom_call_target="tpu_custom_call" | custom-call | bytes 4194304 | tf_op jit(solution)/shard_map/pallas_call | solution.py:171
  2.5 8.5 %all-to-all-start = ((bf16[8,192,512]{2,1,0:T(8,128)(2,1)}), bf16[8,192,512]{2,1,0:T(8,128)(2,1)S(1)}, u32[]{:S(2)}, u32[]{:S(2)}) async-start(bf16[8,192,512]{2,1,0:T(8,128)(2,1)} %shard_map.64), calls=%async_computation | async-start | bytes 3145728 | tf_op jit(solution)/shard_map/all_to_all | solution.py:248
  10.9 0.9 constant_dynamic-slice_fusion
  11.9 2.8 %collective-permute-start.2 = (bf16[256,256]{1,0:T(8,128)(2,1)S(1)}, bf16[256,256]{1,0:T(8,128)(2,1)S(1)}, u32[]{:S(2)}, u32[]{:S(2)}) collective-permute-start(bf16[256,256]{1,0:T(8,128)(2,1)S(1)} %get-tuple-element.9), channel_id=1, source_target_pairs={{0,192},{64,0},{128,64},{192,128},{1,193},{65,1},{129,65},{193,129... | collective-permute-start | bytes 393224 | tf_op jit(solution)/shard_map/ppermute | solution.py:260
  14.7 0.0 collective-permute-start.1
  14.7 2.3 collective-permute-start.3
  17.0 0.2 collective-permute-done.2
  17.2 6.2 %collective-permute-done.1 = bf16[256,256]{1,0:T(8,128)(2,1)S(1)} collective-permute-done((bf16[256,256]{1,0:T(8,128)(2,1)S(1)}, bf16[256,256]{1,0:T(8,128)(2,1)S(1)}, u32[]{:S(2)}, u32[]{:S(2)}) %collective-permute-start.1) | collective-permute-done | bytes 131104 | tf_op jit(solution)/shard_map/ppermute | solution.py:260
  23.4 0.0 collective-permute-done.3
  23.4 1.4 collective-permute-start.4
  24.9 10.2 %collective-permute-done.4 = bf16[1024,256]{1,0:T(8,128)(2,1)S(1)} collective-permute-done((bf16[1024,256]{1,0:T(8,128)(2,1)S(1)}, bf16[1024,256]{1,0:T(8,128)(2,1)S(1)}, u32[]{:S(2)}, u32[]{:S(2)}) %collective-permute-start.4) | collective-permute-done | bytes 524320 | tf_op jit(solution)/shard_map/ppermute | solution.py:233
  35.1 0.1 collective-permute-start.5
  35.9 0.1 pad_add_fusion.meta
  36.0 14.9 %all-to-all-done = bf16[8,192,512]{2,1,0:T(8,128)(2,1)S(1)} async-done(((bf16[8,192,512]{2,1,0:T(8,128)(2,1)}), bf16[8,192,512]{2,1,0:T(8,128)(2,1)S(1)}, u32[]{:S(2)}, u32[]{:S(2)}) %all-to-all-start) | async-done | bytes 1572896 | tf_op jit(solution)/shard_map/all_to_all | solution.py:248
  50.9 0.1 slice.4
  51.0 0.4 collective-permute-start
  51.4 0.0 collective-permute-done.5.prefix_b
  51.4 16.0 %shard_map.65 = (f32[2,1536,128]{2,1,0:T(8,128)S(1)}, f32[2,1536,256]{2,1,0:T(8,128)S(1)}) custom-call(bf16[1536,512]{1,0:T(8,128)(2,1)S(1)} %bitcast.8, bf16[2048,256]{1,0:T(8,128)(2,1)S(1)} %constant_dynamic-update-slice_fusion.prefix_a, bf16[2048,256]{1,0:T(8,128)(2,1)} %collective-permute-done.5.prefix_b), custom_call_target="tpu_custom_call" | custom-call | flops 12884901888 | bytes 4194304 | tf_op jit(solution)/shard_map/pallas_call | solution.py:171
  67.4 2.5 %collective-permute-done.other = bf16[1536,256]{1,0:T(8,128)(2,1)S(1)} collective-permute-done((bf16[1536,256]{1,0:T(8,128)(2,1)S(1)}, bf16[1536,256]{1,0:T(8,128)(2,1)S(1)}, u32[]{:S(2)}, u32[]{:S(2)}) %collective-permute-start) | collective-permute-done | bytes 786464 | tf_op jit(solution)/shard_map/ppermute | solution.py:233
  69.9 146.1 %shard_map.66 = bf16[1536,256]{1,0:T(8,128)(2,1)S(1)} custom-call(s32[2]{0:T(128)S(1)} %pad_add_fusion.meta, bf16[1536,512]{1,0:T(8,128)(2,1)S(1)} %bitcast.9, bf16[1536,256]{1,0:T(8,128)(2,1)S(1)} %collective-permute-done.other, f32[2,1536,128]{2,1,0:T(8,128)S(1)} %get-tuple-element.7.shifts, f32[2,1536,256]{2,1,0:T(8,128)S(1)} %get-tuple-element.8.accum, ...), custom_call_target="tpu_custom_call" | custom-call | flops 4831838208 | bytes 4194304 | tf_op jit(solution)/shard_map/pallas_call | solution.py:171
  215.9 25.9 %all_to_all.10.by_head = bf16[8,192,256]{2,1,0:T(8,128)(2,1)S(1)} all-to-all(bf16[8,192,256]{2,1,0:T(8,128)(2,1)S(1)} %bitcast.10), channel_id=1, replica_groups=mesh['x'=4,'yl'=2,'core'=2,'z'=8,'yh'=2] {'z'}, dimensions={0} | all-to-all | bytes 1572864 | tf_op jit(solution)/shard_map/all_to_all | solution.py:283
  241.8 1.0 shard_map.67
  (6 shorter events, 0.1 us)
Async XLA Ops:
  2.5 48.4 %all-to-all-start = ((bf16[8,192,512]{2,1,0:T(8,128)(2,1)}), bf16[8,192,512]{2,1,0:T(8,128)(2,1)S(1)}, u32[]{:S(2)}, u32[]{:S(2)}) async-start(bf16[8,192,512]{2,1,0:T(8,128)(2,1)} %shard_map.64), calls=%async_computation | async-start | bytes 3145728 | tf_op jit(solution)/shard_map/all_to_all | solution.py:248
  11.9 5.4 %collective-permute-start.2 = (bf16[256,256]{1,0:T(8,128)(2,1)S(1)}, bf16[256,256]{1,0:T(8,128)(2,1)S(1)}, u32[]{:S(2)}, u32[]{:S(2)}) collective-permute-start(bf16[256,256]{1,0:T(8,128)(2,1)S(1)} %get-tuple-element.9), channel_id=1, source_target_pairs={{0,192},{64,0},{128,64},{192,128},{1,193},{65,1},{129,65},{193,129... | collective-permute-start | bytes 393224 | tf_op jit(solution)/shard_map/ppermute | solution.py:260
  14.7 8.7 %collective-permute-start.1 = (bf16[256,256]{1,0:T(8,128)(2,1)S(1)}, bf16[256,256]{1,0:T(8,128)(2,1)S(1)}, u32[]{:S(2)}, u32[]{:S(2)}) collective-permute-start(bf16[256,256]{1,0:T(8,128)(2,1)S(1)} %get-tuple-element.9), channel_id=1, source_target_pairs={{0,64},{64,128},{128,192},{192,0},{1,65},{65,129},{129,193},{193,1... | collective-permute-start | bytes 393224 | tf_op jit(solution)/shard_map/ppermute | solution.py:260
  14.7 8.7 %collective-permute-start.3 = (bf16[256,256]{1,0:T(8,128)(2,1)S(1)}, bf16[256,256]{1,0:T(8,128)(2,1)S(1)}, u32[]{:S(2)}, u32[]{:S(2)}) collective-permute-start(bf16[256,256]{1,0:T(8,128)(2,1)S(1)} %get-tuple-element.9), channel_id=1, source_target_pairs={{0,128},{64,192},{128,0},{192,64},{1,129},{65,193},{129,1},{193,65... | collective-permute-start | bytes 393224 | tf_op jit(solution)/shard_map/ppermute | solution.py:260
  23.4 11.7 %collective-permute-start.4 = (bf16[1024,256]{1,0:T(8,128)(2,1)S(1)}, bf16[1024,256]{1,0:T(8,128)(2,1)S(1)}, u32[]{:S(2)}, u32[]{:S(2)}) collective-permute-start(bf16[1024,256]{1,0:T(8,128)(2,1)S(1)} %pad_maximum_fusion), channel_id=1, source_target_pairs={{0,32},{32,0},{1,33},{33,1},{2,34},{34,2},{3,35},{35,3},{4,36},{36... | collective-permute-start | bytes 1572872 | tf_op jit(solution)/shard_map/ppermute | solution.py:233
  35.1 16.2 %collective-permute-start.5 = (bf16[2048,256]{1,0:T(8,128)(2,1)S(1)}, bf16[2048,256]{1,0:T(8,128)(2,1)}, u32[]{:S(2)}, u32[]{:S(2)}) collective-permute-start(bf16[2048,256]{1,0:T(8,128)(2,1)S(1)} %constant_dynamic-update-slice_fusion.prefix_a), channel_id=1, source_target_pairs={{0,16},{16,0},{1,17},{17,1},{2,18},{18,2},{3,19},{19,3},{4,20},{20... | collective-permute-start | bytes 3145736 | tf_op jit(solution)/shard_map/ppermute | solution.py:233
  51.0 18.9 %collective-permute-start = (bf16[1536,256]{1,0:T(8,128)(2,1)S(1)}, bf16[1536,256]{1,0:T(8,128)(2,1)S(1)}, u32[]{:S(2)}, u32[]{:S(2)}) collective-permute-start(bf16[1536,256]{1,0:T(8,128)(2,1)S(1)} %slice.4), channel_id=1, source_target_pairs={{0,1},{1,0},{2,3},{3,2},{4,5},{5,4},{6,7},{7,6},{8,9},{9,8},{10,11... | collective-permute-start | bytes 2359304 | tf_op jit(solution)/shard_map/ppermute | solution.py:233
